TPU v7x, 32 devices: a whole 2x2x4 slice. The times are simulated.
32 devices in a mesh: rows: 8 (over z, x), seq: 4 (over y, core).
Axes of the slice: x: 2, y: 2, z: 4, core: 2. Of those that a mesh axis runs over, the one named last changes fastest.
Arguments:
- frames_in: bfloat16 [16, 4096, 512], P('rows', 'seq'), may hold values from -6 to 6
- lengths: int32 [16, 4], P('rows'), may hold values from 1 to 2048, 4096 in all within a row
- bw_ids: int32 [16, 4], P('rows'), may hold values from 0 to 3
- owner_list: int32 [137], replicated, may hold values from 0 to 7, as said below
- master: float32 [216, 32, 512], P('rows')
- moment1: float32 [216, 32, 512], P('rows')
- moment2: float32 [216, 32, 512], P('rows'), as said below
- wave_grad: bfloat16 [16, 1310720], P('rows', 'seq'), may hold values from -6 to 6
Outputs:
- waveform: float32 [16, 1310720], P('rows', 'seq')
- input_grad: float32 [16, 4096, 512], P('rows', 'seq')
- new_master: float32 [216, 32, 512], P('rows')
- new_moment1: float32 [216, 32, 512], P('rows')
- new_moment2: float32 [216, 32, 512], P('rows')
Inputs may be any that keep to these rules, and one draw needn't show every extreme that they name: `owner_list`: no index along rows owns more than 27 buckets, and some index owns exactly 27. `moment2`: every entry is positive.
All inputs are finite; a program needn't handle non-finite values.
Results may differ from a plain program's by a relative error of at most 0.012.
The roundings to bfloat16 on the way count: a program that leaves them out, or rounds other values in their place, can miss the bound.
Values may be sent and summed in bfloat16 or wider, within the bound.
No kernel may reach another device: no remote copies, remote signals or barrier semaphores. Data moves between devices by JAX's collectives and lax.ppermute only.
A program may use at most 192 MiB of HBM per device.

v0:
```python
import math
import jax
import jax.numpy as jnp
from jax import lax
from jax.sharding import PartitionSpec as P

FF = 1536
NFFT = 1280
HOP = 320
NBW = 4
KW = 7
UTT = 4
BR = 32
STEP_COUNT = 6
BINS = 641
NOUT = 1282
VROWS = 20
IN_ROWS = 3
HEAD_ROWS = 3
PR = 4380
NB = 137
NORM_EPS = 1e-06
ENV_FLOOR = 0.5
BETA_ONE = 0.8
BETA_TWO = 0.9
LEARN_RATE = 0.04
WEIGHT_DECAY = 0.01
ADAM_EPS = 1e-08


def padded(block, sides, width):
    for axis, dim in sides:
        count = lax.axis_size(axis)
        forward = [(i, i + 1) for i in range(count - 1)]
        backward = [(target, source) for source, target in forward]
        low = lax.ppermute(
            lax.slice_in_dim(block, block.shape[dim] - width, None, axis=dim), axis, forward
        )
        high = lax.ppermute(lax.slice_in_dim(block, 0, width, axis=dim), axis, backward)
        block = jnp.concatenate([low, block, high], axis=dim)
    return block


def from_behind(block, axis, distance):
    devices = range(lax.axis_size(axis))
    route = [(i - distance, i) for i in devices if i - distance in devices]
    return lax.ppermute(block, axis, route)


def slot_maps(owner_list, owner_count, slot_count):
    bucket_count = owner_list.shape[0]
    bucket_index = jnp.arange(bucket_count, dtype=jnp.int32)
    same_owner = owner_list[None, :] == owner_list[:, None]
    before = bucket_index[None, :] < bucket_index[:, None]
    slot_rank = jnp.sum((same_owner & before).astype(jnp.int32), axis=1)
    bucket_place = owner_list * slot_count + slot_rank
    targets = jnp.arange(owner_count * slot_count, dtype=jnp.int32)
    slot_match = bucket_place[None, :] == targets[:, None]
    found_bucket = jnp.sum(slot_match.astype(jnp.int32) * bucket_index[None, :], axis=1)
    source = jnp.where(jnp.any(slot_match, axis=1), found_bucket, bucket_count)
    return (bucket_place, source)


def synthesis_table():
    bin_index = jnp.arange(BINS, dtype=jnp.int32)[:, None]
    tap_index = jnp.arange(NFFT, dtype=jnp.int32)[None, :]
    turns = bin_index * tap_index % NFFT
    angle = turns.astype(jnp.float32) * (2.0 * math.pi / NFFT)
    edge_bin = (bin_index == 0) | (bin_index == NFFT // 2)
    factor = jnp.where(edge_bin, 1.0, 2.0).astype(jnp.float32) / NFFT
    return jnp.concatenate([factor * jnp.cos(angle), -factor * jnp.sin(angle)], axis=0)


def hann_window():
    angle = jnp.arange(NFFT, dtype=jnp.int32).astype(jnp.float32) * (2.0 * math.pi / NFFT)
    return 0.5 - 0.5 * jnp.cos(angle)


def segment_ids(lengths, first_index, span):
    starts = jnp.cumsum(lengths, axis=1) - lengths
    frame_index = first_index + jnp.arange(span, dtype=jnp.int32)
    return jnp.sum((starts[:, None, :] <= frame_index[None, :, None]).astype(jnp.int32), axis=2) - 1


def layer_norm(values):
    row_mean = jnp.mean(values, axis=-1, keepdims=True)
    centered = values - row_mean
    return centered * lax.rsqrt(jnp.mean(centered * centered, axis=-1, keepdims=True) + NORM_EPS)


def ada_norm(values, scale_rows, shift_rows):
    return layer_norm(values) * scale_rows + shift_rows


def final_norm(values, norm_gain, norm_bias):
    return layer_norm(values) * norm_gain[None, :] + norm_bias[None, :]


def exact_gelu(values):
    return jax.nn.gelu(values, approximate=False)


def contract(left_side, right_side, left_dim, right_dim):
    return lax.dot_general(
        left_side,
        right_side,
        (((left_dim,), (right_dim,)), ((), ())),
        preferred_element_type=jnp.float32,
    )


def local(frames_in, lengths, bw_ids, owner_list, master, moment1, moment2, wave_grad):
    rows_here, frames_here, channels = frames_in.shape
    slot_count = master.shape[0]
    frame_count = rows_here * frames_here
    lap_count = NFFT // HOP
    rim_width = (KW - 1) // 2
    margin = max(rim_width, lap_count - 1)
    bucket_place, source = slot_maps(owner_list, lax.axis_size("rows"), slot_count)
    gathered = lax.all_gather(master.astype(jnp.bfloat16), "rows", axis=0, tiled=True)
    buckets = jnp.take(gathered, bucket_place, axis=0)
    weight_table = buckets.reshape(-1, channels)[:PR]
    w_in = weight_table[:FF]
    w_out = weight_table[FF : 2 * FF]
    w_head = weight_table[2 * FF : 2 * FF + NOUT]
    row_start = 2 * FF + NOUT
    channel_rows = weight_table[row_start : row_start + VROWS].astype(jnp.float32)
    row_start = row_start + VROWS
    bias_in = weight_table[row_start : row_start + IN_ROWS].reshape(-1).astype(jnp.float32)
    row_start = row_start + IN_ROWS
    bias_head = (
        weight_table[row_start : row_start + HEAD_ROWS].reshape(-1)[:NOUT].astype(jnp.float32)
    )
    conv_weight = channel_rows[:KW]
    conv_bias = channel_rows[KW]
    ada_scale = channel_rows[KW + 1 : KW + 1 + NBW]
    ada_shift = channel_rows[KW + 1 + NBW : KW + 1 + 2 * NBW]
    vec_base = KW + 1 + 2 * NBW
    bias_out = channel_rows[vec_base]
    layer_scale = channel_rows[vec_base + 1]
    norm_gain = channel_rows[vec_base + 2]
    norm_bias = channel_rows[vec_base + 3]
    first_index = lax.axis_index("seq") * frames_here - margin
    segment = segment_ids(lengths, first_index, frames_here + 2 * margin)
    own_segment = segment[:, margin : margin + frames_here]
    halo_frames = padded(frames_in, (("seq", 1),), rim_width)
    wide_frames = halo_frames.astype(jnp.float32)
    conv_keep = []
    conv_out = jnp.zeros((rows_here, frames_here, channels), jnp.float32) + conv_bias
    for tap_index in range(KW):
        lower = margin - rim_width + tap_index
        keep = (segment[:, lower : lower + frames_here] == own_segment).astype(jnp.float32)[
            :, :, None
        ]
        conv_keep.append(keep)
        conv_out = (
            conv_out
            + keep * wide_frames[:, tap_index : tap_index + frames_here] * conv_weight[tap_index]
        )
    conv_out = conv_out.reshape(frame_count, channels)
    utt_pick = (own_segment[:, :, None] == jnp.arange(UTT, dtype=jnp.int32)[None, None, :]).astype(
        jnp.int32
    )
    frame_ids = jnp.sum(utt_pick * bw_ids[:, None, :], axis=2).reshape(frame_count)
    bw_onehot = (frame_ids[:, None] == jnp.arange(NBW, dtype=jnp.int32)[None, :]).astype(
        jnp.float32
    )
    scale_rows = jnp.dot(bw_onehot, ada_scale, precision=lax.Precision.HIGHEST)
    shift_rows = jnp.dot(bw_onehot, ada_shift, precision=lax.Precision.HIGHEST)
    ada_value, ada_back = jax.vjp(ada_norm, conv_out, scale_rows, shift_rows)
    ada_low = ada_value.astype(jnp.bfloat16)
    hidden_pre = contract(ada_low, w_in, 1, 1) + bias_in[None, :]
    act_value, gelu_back = jax.vjp(exact_gelu, hidden_pre)
    act_low = act_value.astype(jnp.bfloat16)
    branch = contract(act_low, w_out, 1, 0) + bias_out[None, :]
    frames_flat = frames_in.reshape(frame_count, channels).astype(jnp.float32)
    residual = frames_flat + layer_scale[None, :] * branch
    normed_value, final_back = jax.vjp(final_norm, residual, norm_gain, norm_bias)
    normed_low = normed_value.astype(jnp.bfloat16)
    head_out = contract(normed_low, w_head, 1, 1) + bias_head[None, :]
    magnitude = jnp.exp(head_out[:, :BINS])
    phase_angle = head_out[:, BINS:]
    real_part = magnitude * jnp.cos(phase_angle)
    imag_part = magnitude * jnp.sin(phase_angle)
    spectrum_low = jnp.concatenate([real_part, imag_part], axis=1).astype(jnp.bfloat16)
    synthesis = synthesis_table().astype(jnp.bfloat16)
    signal = contract(spectrum_low, synthesis, 1, 0)
    window_rows = hann_window().reshape(lap_count, HOP)
    pieces = signal.reshape(rows_here, frames_here, lap_count, HOP) * window_rows[None, None, :, :]
    lap_keep = []
    numerator = jnp.zeros((rows_here, frames_here + lap_count - 1, HOP), jnp.float32)
    envelope = jnp.zeros((rows_here, frames_here, HOP), jnp.float32)
    for lap_index in range(lap_count):
        ahead = margin + lap_index
        keep = (segment[:, ahead : ahead + frames_here] == own_segment).astype(jnp.float32)[
            :, :, None
        ]
        lap_keep.append(keep)
        numerator = numerator + jnp.pad(
            keep * pieces[:, :, lap_index], ((0, 0), (lap_index, lap_count - 1 - lap_index), (0, 0))
        )
        behind = margin - lap_index
        back_keep = (segment[:, behind : behind + frames_here] == own_segment).astype(jnp.float32)[
            :, :, None
        ]
        envelope = envelope + back_keep * (window_rows[lap_index] ** 2)[None, None, :]
    arrived = from_behind(numerator[:, frames_here:], "seq", 1)
    numerator = numerator[:, :frames_here] + jnp.pad(
        arrived, ((0, 0), (0, frames_here - lap_count + 1), (0, 0))
    )
    denominator = jnp.maximum(envelope, ENV_FLOOR)
    waveform = (numerator / denominator).reshape(rows_here, frames_here * HOP)
    scaled = wave_grad.astype(jnp.float32).reshape(rows_here, frames_here, HOP) / denominator
    later_rows = from_behind(scaled[:, : lap_count - 1], "seq", -1)
    reach_rows = jnp.concatenate([scaled, later_rows], axis=1)
    signal_grad = jnp.stack(
        [
            lap_keep[lap_index]
            * window_rows[lap_index][None, None, :]
            * reach_rows[:, lap_index : lap_index + frames_here]
            for lap_index in range(lap_count)
        ],
        axis=2,
    )
    signal_low = signal_grad.reshape(frame_count, NFFT).astype(jnp.bfloat16)
    spec_grad = contract(signal_low, synthesis, 1, 1)
    real_grad = spec_grad[:, :BINS]
    imag_grad = spec_grad[:, BINS:]
    head_grad = jnp.concatenate(
        [
            real_grad * real_part + imag_grad * imag_part,
            imag_grad * real_part - real_grad * imag_part,
        ],
        axis=1,
    ).astype(jnp.bfloat16)
    grad_w_head = contract(head_grad, normed_low, 0, 0)
    grad_b_head = jnp.sum(head_grad, axis=0, dtype=jnp.float32)
    normed_grad = contract(head_grad, w_head, 1, 0)
    residual_grad, grad_gain, grad_bias = final_back(normed_grad)
    branch_low = (layer_scale[None, :] * residual_grad).astype(jnp.bfloat16)
    grad_layer_scale = jnp.sum(residual_grad * branch, axis=0)
    grad_w_out = contract(act_low, branch_low, 0, 0)
    grad_b_out = jnp.sum(branch_low, axis=0, dtype=jnp.float32)
    act_grad = contract(branch_low, w_out, 1, 1)
    pre_low = gelu_back(act_grad)[0].astype(jnp.bfloat16)
    grad_w_in = contract(pre_low, ada_low, 0, 0)
    grad_b_in = jnp.sum(pre_low, axis=0, dtype=jnp.float32)
    ada_grad = contract(pre_low, w_in, 1, 0)
    conv_grad, scale_grad_rows, shift_grad_rows = ada_back(ada_grad)
    grad_scales = lax.dot_general(
        bw_onehot, scale_grad_rows, (((0,), (0,)), ((), ())), precision=lax.Precision.HIGHEST
    )
    grad_shifts = lax.dot_general(
        bw_onehot, shift_grad_rows, (((0,), (0,)), ((), ())), precision=lax.Precision.HIGHEST
    )
    conv_rows = conv_grad.reshape(rows_here, frames_here, channels)
    grad_conv_b = jnp.sum(conv_grad, axis=0)
    grad_conv_w = jnp.stack(
        [
            jnp.sum(
                conv_keep[tap_index]
                * conv_rows
                * wide_frames[:, tap_index : tap_index + frames_here],
                axis=(0, 1),
            )
            for tap_index in range(KW)
        ],
        axis=0,
    )
    halo_grad = padded(conv_rows, (("seq", 1),), rim_width)
    input_grad = residual_grad.reshape(rows_here, frames_here, channels)
    for tap_index in range(KW):
        lower = margin + rim_width - tap_index
        keep = (segment[:, lower : lower + frames_here] == own_segment).astype(jnp.float32)[
            :, :, None
        ]
        begin = 2 * rim_width - tap_index
        input_grad = (
            input_grad + conv_weight[tap_index] * keep * halo_grad[:, begin : begin + frames_here]
        )
    vec_grads = jnp.concatenate(
        [
            grad_conv_w,
            grad_conv_b[None, :],
            grad_scales,
            grad_shifts,
            jnp.stack([grad_b_out, grad_layer_scale, grad_gain, grad_bias], axis=0),
        ],
        axis=0,
    )
    in_rows = grad_b_in.reshape(IN_ROWS, channels)
    head_rows = jnp.pad(grad_b_head, (0, HEAD_ROWS * channels - NOUT)).reshape(HEAD_ROWS, channels)
    grad_table = jnp.concatenate(
        [grad_w_in, grad_w_out, grad_w_head, vec_grads, in_rows, head_rows], axis=0
    )
    grad_buckets = jnp.pad(grad_table, ((0, NB * BR - PR), (0, 0))).reshape(NB, BR, channels)
    empty_bucket = jnp.zeros((1, BR, channels), jnp.float32)
    summed = lax.psum(grad_buckets, ("rows", "seq"))
    extended = jnp.concatenate([summed, empty_bucket], axis=0)
    my_sources = lax.dynamic_slice_in_dim(source, lax.axis_index("rows") * slot_count, slot_count)
    reduced = jnp.take(extended, my_sources, axis=0)
    first_new = BETA_ONE * moment1 + (1.0 - BETA_ONE) * reduced
    second_new = BETA_TWO * moment2 + (1.0 - BETA_TWO) * reduced * reduced
    first_fix = 1.0 - BETA_ONE**STEP_COUNT
    second_fix = 1.0 - BETA_TWO**STEP_COUNT
    master_new = master - LEARN_RATE * (
        first_new / first_fix / (jnp.sqrt(second_new / second_fix) + ADAM_EPS)
        + WEIGHT_DECAY * master
    )
    return (waveform, input_grad, master_new, first_new, second_new)


def solution(mesh):
    in_specs = (
        P("rows", "seq", None),
        P("rows", None),
        P("rows", None),
        P(),
        P("rows", None, None),
        P("rows", None, None),
        P("rows", None, None),
        P("rows", "seq"),
    )
    out_specs = (
        P("rows", "seq"),
        P("rows", "seq", None),
        P("rows", None, None),
        P("rows", None, None),
        P("rows", None, None),
    )
    return jax.shard_map(local, mesh=mesh, in_specs=in_specs, out_specs=out_specs, check_vma=False)
```

profile of v0, /device:TPU:0, one launch (start us, length us, event | category | flops | bytes accessed | tf_op | source)
XLA Modules:
  0.0 546.3 jit_solution(15566940357598605938)
XLA Ops:
  7.2 2.5 convert_element_type.160
  10.6 2.4 collective-permute-start
  12.9 1.3 collective-permute-start.1
  15.8 2.7 reshape.271
  18.5 2.2 copy.39
  21.1 2.9 fusion.48
  24.8 1.3 collective-permute-start.3
  26.2 2.7 reshape.270
  28.9 2.2 copy.37
  33.0 2.8 fusion.47
  35.9 15.2 %multiply_convert_fusion.2 = (bf16[641,1280]{1,0:T(8,128)(2,1)}, bf16[641,1280]{1,0:T(8,128)(2,1)}) fusion(f32[641]{0:T(1024)S(1)} %fusion.74, f32[641]{0:T(1024)S(1)} %select_multiply_fusion), kind=kLoop, calls=%fused_computation.89 | loop fusion | flops 10666240 | bytes 3287048 | tf_op jit(solution)/shard_map/convert.12
  51.9 9.4 %concatenate.35 = bf16[2,1030,512]{2,1,0:T(8,128)(2,1)S(1)} concatenate(bf16[2,3,512]{2,1,0:T(4,128)(2,1)S(1)} %collective-permute-done, bf16[2,1024,512]{2,1,0:T(8,128)(2,1)} %param.8, bf16[2,3,512]{2,1,0:T(4,128)(2,1)S(1)} %collective-permute-done.1), dimensions={1} | concatenate | bytes 4218880 | tf_op jit(solution)/shard_map/concatenate | solution.py:40
  61.3 2.6 convert_element_type.164
  63.8 4.7 fusion.55
  68.5 3.2 pad_maximum_fusion.1
  71.7 10.2 %copy.40 = bf16[2,1024,4,320]{1,0,3,2:T(2,128)(2,1)} copy(bf16[2,1024,4,320]{1,3,0,2:T(8,128)(2,1)} %pad_maximum_fusion.1) | data formatting | bytes 10485760 | tf_op jit(solution)/shard_map/stack | solution.py:216
  81.9 4.8 copy.45
  86.7 9.7 %fusion.49 = f32[2048,1282]{0,1:T(8,128)} fusion(bf16[2048,1280]{0,1:T(8,128)(2,1)S(1)} %bitcast.122, bf16[641,1280]{1,0:T(8,128)(2,1)S(1)} %copy-done.20, bf16[641,1280]{1,0:T(8,128)(2,1)S(1)} %copy-done.21), kind=kOutput, calls=%fused_computation.122 | convolution fusion | flops 6727936000 | bytes 19026944 | tf_op jit(solution)/shard_map/dot_general | solution.py:104
  96.5 25.9 %all-gather.2.cloned.1.call-done = bf16[216,32,512]{2,1,0:T(8,128)(2,1)} async-done(((bf16[27,32,512]{2,1,0:T(8,128)(2,1)}), bf16[216,32,512]{2,1,0:T(8,128)(2,1)}) %all-gather.2.cloned.1.call-update) | async-done | bytes 7077904 | tf_op jit(solution)/shard_map/all_gather | solution.py:120
  122.3 10.9 %gather_fusion = bf16[137,32,512]{2,1,0:T(8,128)(2,1)} fusion(bf16[216,32,512]{2,1,0:T(8,128)(2,1)} %all-gather.2.cloned.1.call-done, s32[1024]{0:T(1024)S(1)} %pad_clamp_fusion.1), kind=kCustom, calls=%fused_computation | custom fusion | bytes 8978980 | tf_op jit(solution)/shard_map/jit(_take)/gather | solution.py:121
  133.3 4.1 bitcast_select_fusion
  137.5 2.6 broadcast_select_fusion
  140.2 2.4 slice-done
  142.7 6.1 %fusion.88 = (f32[2,1024]{1,0:T(2,128)S(1)}, f32[2,1024,512]{2,1,0:T(8,128)S(1)}) fusion(f32[512]{0:T(512)S(1)} %bitcast.134, f32[2,1030,512]{2,1,0:T(8,128)S(1)} %bitcast.114, f32[2,1024]{1,0:T(2,128)S(1)} %get-tuple-element.69, f32[512]{0:T(512)S(1)} %bitcast.136, f32[2,1024]{1,0:T(2,128)S(1)} %get-tuple-element.70, f32[512]{0:T(512)S(1)} %bitcast.138, ...), kind=kLoop, calls=%fused_computation.211 | loop fusion | flops 22018048 | bytes 33628160 | tf_op jit(solution)/shard_map/jvp()/reduce_sum | solution.py:86
  149.7 2.4 bitcast_subtract_fusion
  152.1 2.5 fusion.60
  154.7 2.3 fusion.89
  157.8 4.0 add_convert_fusion.3
  161.8 31.4 %multiply_convert_fusion = (bf16[2048,1536]{1,0:T(8,128)(2,1)S(1)}, f32[2048,1536]{1,0:T(8,128)}, f32[2048,1536]{1,0:T(8,128)}) fusion(f32[1536]{0:T(1024)S(1)} %reshape.280, bf16[2048,512]{1,0:T(8,128)(2,1)S(1)} %add_convert_fusion.3, bf16[1536,512]{1,0:T(8,128)(2,1)S(1)} %bitcast.123), kind=kOutput, calls=%fused_computation.6 | convolution fusion | flops 3428843520 | bytes 35133440 | tf_op jit(solution)/shard_map/dot_general | solution.py:104
  193.2 5.6 %fusion.86 = (f32[2048]{0:T(1024)S(1)}, f32[2048,512]{1,0:T(8,128)S(1)}, f32[2048,512]{1,0:T(8,128)}) fusion(f32[512]{0:T(512)S(1)} %bitcast.159, f32[512]{0:T(512)S(1)} %bitcast.157, bf16[2,1024,512]{2,1,0:T(8,128)(2,1)S(1)} %copy-done.16, bf16[2048,1536]{1,0:T(8,128)(2,1)S(1)} %get-tuple-element.32, bf16[1536,512]{1,0:T(8,128)(2,1)S(1)} %bitcast.125), kind=kOutput, calls=%fused_computation.210 | convolution fusion | flops 3226466304 | bytes 18362368 | tf_op jit(solution)/shard_map/dot_general | solution.py:104
  198.8 1.9 copy-done.8
  201.6 5.8 %convolution_add_fusion = f32[2048,1282]{0,1:T(8,128)S(1)} fusion(f32[1282]{0:T(1024)S(1)} %slice_convert_fusion.1, bf16[4384,512]{1,0:T(8,128)(2,1)} %copy-done.13, f32[2048,512]{1,0:T(8,128)} %copy-done.8, f32[512]{0:T(512)S(1)} %bitcast.169, f32[512]{0:T(512)S(1)} %bitcast.163, f32[2048]{0:T(1024)S(1)} %fusion.70, f32[2048]{0:T(1024)S(1)} %broadcast_multiply_fusion), kind=kOutput, calls=%fused_computation.22 | convolution fusion | flops 2696417280 | bytes 16040968 | tf_op jit(solution)/shard_map/dot_general | solution.py:104
  207.5 24.2 %add_convert_fusion.1 = (bf16[2048,641]{0,1:T(8,128)(2,1)S(1)}, bf16[2048,641]{0,1:T(8,128)(2,1)S(1)}, bf16[2048,641]{0,1:T(8,128)(2,1)}, bf16[2048,641]{0,1:T(8,128)(2,1)}) fusion(f32[2048,1282]{0,1:T(8,128)} %fusion.49, f32[2048,1282]{0,1:T(8,128)S(1)} %convolution_add_fusion), kind=kLoop, calls=%fused_computation.31 | loop fusion | flops 15753216 | bytes 31506432 | tf_op jit(solution)/shard_map/convert.2
  231.7 1.3 convert_reduce_fusion.1
  233.9 6.2 %multiply_reduce_fusion = (f32[512]{0:T(512)S(1)}, f32[2048]{0:T(1024)S(1)}, f32[512]{0:T(512)S(1)}, f32[2048,512]{1,0:T(8,128)S(1)}) fusion(f32[2048,512]{1,0:T(8,128)S(1)} %copy-done.9, f32[2048]{0:T(1024)S(1)} %fusion.70, f32[2048]{0:T(1024)S(1)} %broadcast_multiply_fusion, f32[512]{0:T(512)S(1)} %bitcast.164, bf16[4384,512]{1,0:T(8,128)(2,1)} %copy-done.13, ...), kind=kOutput, calls=%fused_computation.64 | convolution fusion | flops 2707436544 | bytes 14989312 | tf_op jit(solution)/shard_map/dot_general | solution.py:104
  240.1 4.6 fusion.52
  244.7 2.0 fusion.85
  249.5 3.6 fusion.95
  253.1 16.6 %convert_reduce_fusion = (f32[1536]{0:T(1024)S(1)}, bf16[2048,1536]{1,0:T(8,128)(2,1)}) fusion(f32[2048,1536]{1,0:T(8,128)} %get-tuple-element.33, bf16[2048,512]{1,0:T(8,128)(2,1)} %copy-done.19, bf16[1536,512]{1,0:T(8,128)(2,1)} %bitcast.126, f32[2048,1536]{1,0:T(8,128)} %get-tuple-element.84, f32[1536]{0:T(1024)S(1)} %reshape.280), kind=kOutput, calls=%fused_computation.4 | convolution fusion | flops 3274701312 | bytes 35139584 | tf_op jit(solution)/shard_map/dot_general | solution.py:104
  269.7 6.7 %multiply_reduce_fusion.9 = (f32[2048]{0:T(1024)S(1)}, f32[2048,512]{1,0:T(8,128)S(1)}) fusion(f32[2048,512]{1,0:T(8,128)S(1)} %copy-done.4, f32[2048,512]{1,0:T(8,128)S(1)} %copy-done.6, bf16[2048,1536]{1,0:T(8,128)(2,1)} %get-tuple-element.90, bf16[1536,512]{1,0:T(8,128)(2,1)} %bitcast.124), kind=kOutput, calls=%fused_computation.76 | convolution fusion | flops 3224369152 | bytes 20455424 | tf_op jit(solution)/shard_map/dot_general | solution.py:104
  276.4 5.1 fusion.94
  281.5 2.2 fusion.27
  283.7 1.7 fusion.59
  285.5 5.5 %fusion.84 = (f32[2048]{0:T(1024)S(1)}, f32[2048,512]{1,0:T(8,128)S(1)}) fusion(f32[2048]{0:T(1024)S(1)} %fusion.69, f32[2048]{0:T(1024)S(1)} %copy-done.39, f32[2048,512]{1,0:T(8,128)} %copy-done.7, f32[2048,512]{1,0:T(8,128)} %fusion.60, f32[2048]{0:T(1024)S(1)} %bitcast.132, f32[2,1024,512]{2,1,0:T(8,128)} %copy-done), kind=kLoop, calls=%fused_computation.208 | loop fusion | flops 7337984 | bytes 16809984 | tf_op jit(solution)/shard_map/transpose(jvp())/reduce_sum | solution.py:87
  291.5 3.2 slice-done.2
  294.7 5.3 multiply_reduce_fusion.2
  300.1 27.2 %concatenate.42 = f32[4380,512]{1,0:T(8,128)} concatenate(f32[1536,512]{1,0:T(8,128)} %fusion.94, f32[1536,512]{1,0:T(8,128)S(1)} %fusion.95, f32[1282,512]{1,0:T(8,128)} %fusion.52, f32[1,512]{1,0:T(1,128)S(1)} %bitcast.156, f32[1,512]{1,0:T(1,128)S(1)} %bitcast.155, f32[1,512]{1,0:T(1,128)S(1)} %bitcast.154, f32[1,512]{1,0:T(1,128)S(1)} %bitcast.153, f32[1,512]{1,0:T(1,128)S(1)} %bitcast.152, ...), dimensions={0} | concatenate | bytes 17940480 | tf_op jit(solution)/shard_map/concatenate | solution.py:293
  327.2 8.1 %pad.35 = f32[4384,512]{1,0:T(8,128)} pad(f32[4380,512]{1,0:T(8,128)} %concatenate.42, f32[]{:T(128)} %constant.72.clone.1), padding=0_4x0_0 | pad | bytes 17948676 | tf_op jit(solution)/shard_map/jit(_pad)/pad | solution.py:296
  335.3 1.7 copy-done.15
  337.1 13.9 %fusion.6 = f32[2048,1280]{0,1:T(8,128)} fusion(bf16[2048,641]{0,1:T(8,128)(2,1)} %get-tuple-element.41, bf16[2048,641]{0,1:T(8,128)(2,1)S(1)} %copy-done.15, bf16[641,1280]{1,0:T(8,128)(2,1)} %get-tuple-element.91, bf16[641,1280]{1,0:T(8,128)(2,1)} %get-tuple-element.92), kind=kOutput, calls=%fused_computation.34 | convolution fusion | flops 6738438144 | bytes 19018752 | tf_op jit(solution)/shard_map/dot_general | solution.py:104
  350.9 14.4 %reshape.268 = f32[2,1024,4,320]{1,0,3,2:T(2,128)} reshape(f32[2048,1280]{0,1:T(8,128)} %fusion.6) | data formatting | bytes 20971520 | tf_op jit(solution)/shard_map/reshape | solution.py:189
  365.4 8.5 %copy_multiply_fusion = f32[2,1024,4,320]{1,3,0,2:T(8,128)S(1)} fusion(f32[2,1024,4,320]{1,0,3,2:T(2,128)} %reshape.268, f32[4,320]{1,0:T(4,128)S(1)} %copy-done.52), kind=kLoop, calls=%fused_computation.21 | loop fusion | flops 2621440 | bytes 20976640 | tf_op jit(solution)/shard_map/mul | solution.py:189
  374.2 1.8 fusion.46
  376.4 1.5 collective-permute-start.2
  377.9 2.3 pad_add_fusion
  382.3 4.4 collective-permute-start.5
  386.8 2.4 fusion.43
  389.2 2.6 copy.36
  391.9 4.1 reshape.269
  396.1 20.3 %fusion.13 = f32[2,1024,512]{2,1,0:T(8,128)} fusion(f32[2,3,512]{2,1,0:T(4,128)S(1)} %collective-permute-done.5, f32[2,3,512]{2,1,0:T(4,128)S(1)} %collective-permute-done.4, f32[2,1024,512]{2,1,0:T(8,128)} %bitcast.119, f32[2,1024,512]{2,1,0:T(8,128)} %bitcast.118, f32[512]{0:T(512)S(1)} %bitcast.135, f32[2,1024]{1,0:T(2,128)S(1)} %copy-done.31, ...), kind=kLoop, calls=%fused_computation.46 | loop fusion | flops 27262976 | bytes 12670976 | tf_op jit(solution)/shard_map/add | solution.py:279
  416.3 103.8 %all-reduce.10.cloned.1.call-done = f32[137,32,512]{2,1,0:T(8,128)} async-done(((f32[137,32,512]{2,1,0:T(8,128)}), f32[137,32,512]{2,1,0:T(8,128)}) %all-reduce.10.cloned.1.call-update) | async-done | bytes 8978448 | tf_op jit(solution)/shard_map/psum | solution.py:298
  520.2 9.1 %concatenate.43 = f32[138,32,512]{2,1,0:T(8,128)} pad(f32[137,32,512]{2,1,0:T(8,128)} %all-reduce.10.cloned.1.call-done, f32[]{:T(128)} %constant.72.clone.1), padding=0_1x0_0x0_0 | pad | bytes 18022404 | tf_op jit(solution)/shard_map/concatenate | solution.py:299
  529.3 4.5 gather_fusion.1
  533.8 5.5 %multiply_subtract_fusion = (f32[27,32,512]{2,1,0:T(8,128)}, f32[27,32,512]{2,1,0:T(8,128)}, f32[27,32,512]{2,1,0:T(8,128)}) fusion(f32[27,32,512]{2,1,0:T(8,128)S(1)} %copy-done.12, f32[27,32,512]{2,1,0:T(8,128)S(1)} %gather_fusion.1, pred[27]{0:T(512)(128)(4,1)S(1)} %copy-done.68, f32[27,32,512]{2,1,0:T(8,128)} %param.13, f32[27,32,512]{2,1,0:T(8,128)} %param.14), kind=kLoop, calls=%fused_computation.127 | loop fusion | flops 7077888 | bytes 12386331 | tf_op jit(solution)/shard_map/sub | solution.py:306
  (220 shorter events, 16.0 us)
Async XLA Ops:
  7.2 115.2 %all-gather.2.cloned.1.call-start = ((), (), s32[]{:S(2)}) async-start(), calls=%async_computation | async-start | bytes 7962624 | tf_op jit(solution)/shard_map/all_gather | solution.py:120
  9.8 510.4 %all-reduce.10.cloned.1.call-start = ((), (), s32[]{:S(2)}) async-start(), calls=%async_computation.1 | async-start | bytes 17956864 | tf_op jit(solution)/shard_map/psum | solution.py:298
  10.6 41.3 %collective-permute-start = (bf16[2,3,512]{2,1,0:T(4,128)(2,1)S(1)}, bf16[2,3,512]{2,1,0:T(4,128)(2,1)S(1)}, u32[]{:S(2)}, u32[]{:S(2)}) collective-permute-start(bf16[2,3,512]{2,1,0:T(4,128)(2,1)S(1)} %get-tuple-element.55), channel_id=1, source_target_pairs={{0,1},{1,2},{2,3},{4,5},{5,6},{6,7},{8,9},{9,10},{10,11},{12,13},{... | collective-permute-start | bytes 18440 | tf_op jit(solution)/shard_map/ppermute | solution.py:36
  12.9 38.9 %collective-permute-start.1 = (bf16[2,3,512]{2,1,0:T(4,128)(2,1)S(1)}, bf16[2,3,512]{2,1,0:T(4,128)(2,1)S(1)}, u32[]{:S(2)}, u32[]{:S(2)}) collective-permute-start(bf16[2,3,512]{2,1,0:T(4,128)(2,1)S(1)} %get-tuple-element.54), channel_id=1, source_target_pairs={{1,0},{2,1},{3,2},{5,4},{6,5},{7,6},{9,8},{10,9},{11,10},{13,12},{... | collective-permute-start | bytes 18440 | tf_op jit(solution)/shard_map/ppermute | solution.py:39
  20.9 12.1 %copy-start.44 = (f32[320]{0:T(512)}, f32[320]{0:T(512)S(1)}, u32[]{:S(2)}) copy-start(f32[320]{0:T(512)S(1)} %get-tuple-element.75) | copy-start | bytes 3844
  20.9 12.1 %copy-start.46 = (f32[320]{0:T(512)}, f32[320]{0:T(512)S(1)}, u32[]{:S(2)}) copy-start(f32[320]{0:T(512)S(1)} %get-tuple-element.76) | copy-start | bytes 3844
  20.9 12.1 %copy-start.48 = (f32[320]{0:T(512)}, f32[320]{0:T(512)S(1)}, u32[]{:S(2)}) copy-start(f32[320]{0:T(512)S(1)} %get-tuple-element.77) | copy-start | bytes 3844
  20.9 12.1 %copy-start.50 = (f32[320]{0:T(512)}, f32[320]{0:T(512)S(1)}, u32[]{:S(2)}) copy-start(f32[320]{0:T(512)S(1)} %get-tuple-element.78) | copy-start | bytes 3844
  21.1 119.1 %copy-start.24 = (f32[2,1024]{1,0:T(2,128)}, f32[2,1024]{1,0:T(2,128)S(1)}, u32[]{:S(2)}) copy-start(f32[2,1024]{1,0:T(2,128)S(1)} %get-tuple-element.68) | copy-start | bytes 24580
  21.1 119.1 %copy-start.26 = (f32[2,1024]{1,0:T(2,128)}, f32[2,1024]{1,0:T(2,128)S(1)}, u32[]{:S(2)}) copy-start(f32[2,1024]{1,0:T(2,128)S(1)} %get-tuple-element.72) | copy-start | bytes 24580
  21.1 119.1 %copy-start.28 = (f32[2,1024]{1,0:T(2,128)}, f32[2,1024]{1,0:T(2,128)S(1)}, u32[]{:S(2)}) copy-start(f32[2,1024]{1,0:T(2,128)S(1)} %get-tuple-element.73) | copy-start | bytes 24580
  21.1 119.1 %copy-start.30 = (f32[2,1024]{1,0:T(2,128)}, f32[2,1024]{1,0:T(2,128)S(1)}, u32[]{:S(2)}) copy-start(f32[2,1024]{1,0:T(2,128)S(1)} %get-tuple-element.69) | copy-start | bytes 24580
  21.1 119.1 %copy-start.32 = (f32[2,1024]{1,0:T(2,128)}, f32[2,1024]{1,0:T(2,128)S(1)}, u32[]{:S(2)}) copy-start(f32[2,1024]{1,0:T(2,128)S(1)} %get-tuple-element.70) | copy-start | bytes 24580
  21.1 119.1 %copy-start.34 = (f32[2,1024]{1,0:T(2,128)}, f32[2,1024]{1,0:T(2,128)S(1)}, u32[]{:S(2)}) copy-start(f32[2,1024]{1,0:T(2,128)S(1)} %get-tuple-element.71) | copy-start | bytes 24580
  24.8 39.0 %collective-permute-start.3 = (f32[2,3,320]{1,2,0:T(8,128)}, f32[2,3,320]{1,2,0:T(8,128)}, u32[]{:S(2)}, u32[]{:S(2)}) collective-permute-start(f32[2,3,320]{1,2,0:T(8,128)} %slice.387), channel_id=1, source_target_pairs={{1,0},{2,1},{3,2},{5,4},{6,5},{7,6},{9,8},{10,9},{11,10},{13,12},{... | collective-permute-start | bytes 23048 | tf_op jit(solution)/shard_map/ppermute | solution.py:47
  26.2 4.9 copy-start.67
  26.2 6.7 %copy-start.69 = (s32[2,4]{1,0:T(2,128)S(1)}, s32[2,4]{1,0:T(2,128)}, u32[]{:S(2)}) copy-start(s32[2,4]{1,0:T(2,128)} %param.10) | copy-start | bytes 100
  51.8 105.1 %copy-start.36 = (s32[1,8,2,128]{3,1,2,0:T(8,128)}, s32[1,8,2,128]{3,1,2,0:T(8,128)S(1)}, u32[]{:S(2)}) copy-start(s32[1,8,2,128]{3,1,2,0:T(8,128)S(1)} %copy.53) | copy-start | bytes 24580
  81.9 4.8 copy-start.20
  81.9 4.8 copy-start.21
  133.3 4.2 copy-start.1
  137.4 14.7 %copy-start.13 = (bf16[4384,512]{1,0:T(8,128)(2,1)}, bf16[4384,512]{1,0:T(8,128)(2,1)S(1)}, u32[]{:S(2)}) copy-start(bf16[4384,512]{1,0:T(8,128)(2,1)S(1)} %bitcast_select_fusion) | copy-start | bytes 13467652
  137.4 5.3 slice-start
  137.5 5.2 slice-start.1
  140.1 8.7 %copy-start.53 = (f32[1,512]{1,0:T(1,128)}, f32[1,512]{1,0:T(1,128)S(1)}, u32[]{:S(2)}) copy-start(f32[1,512]{1,0:T(1,128)S(1)} %get-tuple-element.59) | copy-start | bytes 6148
  140.1 8.7 %copy-start.55 = (f32[1,512]{1,0:T(1,128)}, f32[1,512]{1,0:T(1,128)S(1)}, u32[]{:S(2)}) copy-start(f32[1,512]{1,0:T(1,128)S(1)} %get-tuple-element.60) | copy-start | bytes 6148
  140.1 8.7 %copy-start.57 = (f32[1,512]{1,0:T(1,128)}, f32[1,512]{1,0:T(1,128)S(1)}, u32[]{:S(2)}) copy-start(f32[1,512]{1,0:T(1,128)S(1)} %get-tuple-element.61) | copy-start | bytes 6148
  140.1 8.7 %copy-start.59 = (f32[1,512]{1,0:T(1,128)}, f32[1,512]{1,0:T(1,128)S(1)}, u32[]{:S(2)}) copy-start(f32[1,512]{1,0:T(1,128)S(1)} %get-tuple-element.62) | copy-start | bytes 6148
  140.2 8.7 %copy-start.61 = (f32[1,512]{1,0:T(1,128)}, f32[1,512]{1,0:T(1,128)S(1)}, u32[]{:S(2)}) copy-start(f32[1,512]{1,0:T(1,128)S(1)} %get-tuple-element.63) | copy-start | bytes 6148
  140.2 8.7 %copy-start.63 = (f32[1,512]{1,0:T(1,128)}, f32[1,512]{1,0:T(1,128)S(1)}, u32[]{:S(2)}) copy-start(f32[1,512]{1,0:T(1,128)S(1)} %get-tuple-element.64) | copy-start | bytes 6148
  140.2 8.7 %copy-start.65 = (f32[1,512]{1,0:T(1,128)}, f32[1,512]{1,0:T(1,128)S(1)}, u32[]{:S(2)}) copy-start(f32[1,512]{1,0:T(1,128)S(1)} %get-tuple-element.65) | copy-start | bytes 6148
  149.7 7.2 %copy-start.38 = (f32[2048]{0:T(1024)}, f32[2048]{0:T(1024)S(1)}, u32[]{:S(2)}) copy-start(f32[2048]{0:T(1024)S(1)} %bitcast_rsqrt_fusion) | copy-start | bytes 24580
  157.8 4.0 copy-start.22
  157.8 35.4 %copy-start.23 = (bf16[48,32,512]{2,1,0:T(8,128)(2,1)}, bf16[48,32,512]{2,1,0:T(8,128)(2,1)S(1)}, u32[]{:S(2)}) copy-start(bf16[48,32,512]{2,1,0:T(8,128)(2,1)S(1)} %get-tuple-element.45) | copy-start | bytes 4718596
  161.8 31.4 %copy-start.17 = (bf16[2048,512]{1,0:T(8,128)(2,1)}, bf16[2048,512]{1,0:T(8,128)(2,1)S(1)}, u32[]{:S(2)}) copy-start(bf16[2048,512]{1,0:T(8,128)(2,1)S(1)} %add_convert_fusion.3) | copy-start | bytes 6291460
  161.8 31.4 %copy-start.16 = (bf16[2,1024,512]{2,1,0:T(8,128)(2,1)S(1)}, bf16[2,1024,512]{2,1,0:T(8,128)(2,1)}, u32[]{:S(2)}) copy-start(bf16[2,1024,512]{2,1,0:T(8,128)(2,1)} %param.8) | copy-start | bytes 6291460
  193.2 5.6 %copy-start.71 = (bf16[2048,1536]{1,0:T(8,128)(2,1)}, bf16[2048,1536]{1,0:T(8,128)(2,1)S(1)}, u32[]{:S(2)}) copy-start(bf16[2048,1536]{1,0:T(8,128)(2,1)S(1)} %get-tuple-element.32) | copy-start | bytes 18874372
  247.5 5.6 %copy-start.5 = (f32[2048,512]{1,0:T(8,128)}, f32[2048,512]{1,0:T(8,128)S(1)}, u32[]{:S(2)}) copy-start(f32[2048,512]{1,0:T(8,128)S(1)} %get-tuple-element.21) | copy-start | bytes 12582916
  248.2 4.9 copy-start.19
  253.1 16.6 %copy-start.4 = (f32[2048,512]{1,0:T(8,128)S(1)}, f32[2048,512]{1,0:T(8,128)}, u32[]{:S(2)}) copy-start(f32[2048,512]{1,0:T(8,128)} %bitcast_subtract_fusion) | copy-start | bytes 12582916
  253.1 16.6 %copy-start.6 = (f32[2048,512]{1,0:T(8,128)S(1)}, f32[2048,512]{1,0:T(8,128)}, u32[]{:S(2)}) copy-start(f32[2048,512]{1,0:T(8,128)} %fusion.60) | copy-start | bytes 12582916
  269.7 6.7 %copy-start.18 = (bf16[2048,512]{1,0:T(8,128)(2,1)S(1)}, bf16[2048,512]{1,0:T(8,128)(2,1)}, u32[]{:S(2)}) copy-start(bf16[2048,512]{1,0:T(8,128)(2,1)} %copy-done.17) | copy-start | bytes 6291460
  269.7 6.7 %copy-start.70 = (bf16[2048,1536]{1,0:T(8,128)(2,1)S(1)}, bf16[2048,1536]{1,0:T(8,128)(2,1)}, u32[]{:S(2)}) copy-start(bf16[2048,1536]{1,0:T(8,128)(2,1)} %get-tuple-element.90) | copy-start | bytes 18874372
  276.4 7.3 %copy-start.7 = (f32[2048,512]{1,0:T(8,128)}, f32[2048,512]{1,0:T(8,128)S(1)}, u32[]{:S(2)}) copy-start(f32[2048,512]{1,0:T(8,128)S(1)} %get-tuple-element.88) | copy-start | bytes 12582916
  276.4 5.1 copy-start.37
  276.4 5.1 copy-start.39
  291.5 8.6 %copy-start.2 = (f32[2048,512]{1,0:T(8,128)}, f32[2048,512]{1,0:T(8,128)S(1)}, u32[]{:S(2)}) copy-start(f32[2048,512]{1,0:T(8,128)S(1)} %get-tuple-element.25) | copy-start | bytes 12582916
  350.9 14.4 %copy-start.52 = (f32[4,320]{1,0:T(4,128)S(1)}, f32[4,320]{1,0:T(4,128)}, u32[]{:S(2)}) copy-start(f32[4,320]{1,0:T(4,128)} %multiply_subtract_fusion.2) | copy-start | bytes 15364
  376.4 10.4 %copy-start.45 = (f32[320]{0:T(512)S(1)}, f32[320]{0:T(512)}, u32[]{:S(2)}) copy-start(f32[320]{0:T(512)} %copy-done.44) | copy-start | bytes 3844
  376.4 10.4 %copy-start.47 = (f32[320]{0:T(512)S(1)}, f32[320]{0:T(512)}, u32[]{:S(2)}) copy-start(f32[320]{0:T(512)} %copy-done.46) | copy-start | bytes 3844
  376.4 10.4 %copy-start.49 = (f32[320]{0:T(512)S(1)}, f32[320]{0:T(512)}, u32[]{:S(2)}) copy-start(f32[320]{0:T(512)} %copy-done.48) | copy-start | bytes 3844
  376.4 10.4 %copy-start.51 = (f32[320]{0:T(512)S(1)}, f32[320]{0:T(512)}, u32[]{:S(2)}) copy-start(f32[320]{0:T(512)} %copy-done.50) | copy-start | bytes 3844
  376.4 10.3 %collective-permute-start.2 = (f32[2,3,320]{1,2,0:T(8,128)S(1)}, f32[2,3,320]{1,2,0:T(8,128)S(1)}, u32[]{:S(2)}, u32[]{:S(2)}) collective-permute-start(f32[2,3,320]{1,2,0:T(8,128)S(1)} %pad_add_fusion.1), channel_id=1, source_target_pairs={{0,1},{1,2},{2,3},{4,5},{5,6},{6,7},{8,9},{9,10},{10,11},{12,13},{... | collective-permute-start | bytes 23048 | tf_op jit(solution)/shard_map/ppermute | solution.py:47
  381.1 14.9 %collective-permute-start.4 = (f32[2,3,512]{2,1,0:T(4,128)S(1)}, f32[2,3,512]{2,1,0:T(4,128)S(1)}, u32[]{:S(2)}, u32[]{:S(2)}) collective-permute-start(f32[2,3,512]{2,1,0:T(4,128)S(1)} %get-tuple-element.49), channel_id=1, source_target_pairs={{1,0},{2,1},{3,2},{5,4},{6,5},{7,6},{9,8},{10,9},{11,10},{13,12},{... | collective-permute-start | bytes 36872 | tf_op jit(solution)/shard_map/ppermute | solution.py:39
  382.3 13.6 %collective-permute-start.5 = (f32[2,3,512]{2,1,0:T(4,128)S(1)}, f32[2,3,512]{2,1,0:T(4,128)S(1)}, u32[]{:S(2)}, u32[]{:S(2)}) collective-permute-start(f32[2,3,512]{2,1,0:T(4,128)S(1)} %get-tuple-element.50), channel_id=1, source_target_pairs={{0,1},{1,2},{2,3},{4,5},{5,6},{6,7},{8,9},{9,10},{10,11},{12,13},{... | collective-permute-start | bytes 36872 | tf_op jit(solution)/shard_map/ppermute | solution.py:36
  391.9 4.1 copy-start.54
  391.9 4.1 copy-start.56
  391.9 4.1 copy-start.58
  391.9 4.1 copy-start.60
  391.9 4.1 copy-start.62
  391.9 4.1 copy-start.64
  391.9 4.1 copy-start.66
  416.3 117.4 %copy-start.68 = (pred[27]{0:T(512)(128)(4,1)S(1)}, pred[27]{0:T(512)(128)(4,1)}, u32[]{:S(2)}) copy-start(pred[27]{0:T(512)(128)(4,1)} %get-tuple-element.18) | copy-start | bytes 85
  529.3 4.5 copy-start.12
  (22 other events, 63.2 us)
Sparse Core Ops, SparseCore 0:
  10.8 111.5 all-gather.1
  335.5 184.6 all-reduce.9
where the time goes:
time: 556 us; the launch traced here: 546 us
  other arithmetic  136 us (24%)
  local copies, waits for them, and re-layouts  133 us (24%)
  waiting for transfers between devices  130 us (23%)
  matrix products  119 us (21%)
  between operations  15.7 us (3%)
  starting transfers between devices  12.2 us (2%)
    dot_general x11, matrix products, contract(): lax.dot_general(left_side, right_side, (((left_dim,), (right_dim,)), ((),...  109 us
    psum x1, waiting for transfers between devices, local(): summed = lax.psum(grad_buckets, ('rows', 'seq'))  104 us
    another operation x3, other arithmetic  42.2 us
    concatenate x1, local copies, waits for them, and re-layouts, local(): jnp.concatenate([grad_w_in, grad_w_out, grad_w_head, vec_grads, in_rows,...  27.2 us
    all_gather x1, waiting for transfers between devices, local(): lax.all_gather(master.astype(jnp.bfloat16), 'rows', axis=0, tiled=True)  25.9 us
    add x1, other arithmetic, local(): input_grad + conv_weight[tap_index] * keep * halo_grad[:, begin:begin + f...  20.3 us
    unnamed x159, local copies, waits for them, and re-layouts  17.5 us
    reshape x1, local copies, waits for them, and re-layouts, local(): signal.reshape(rows_here, frames_here, lap_count, HOP)  14.4 us
  transfers between devices with their start and end apart: 8, of which 2 were waited for; matrix products, arithmetic and copies ran while one was open for 28% of the time, Pallas kernels for 0%

commit v1 on v0

--- a/solution.py
+++ b/solution.py
@@ -117,7 +117,24 @@
     rim_width = (KW - 1) // 2
     margin = max(rim_width, lap_count - 1)
     bucket_place, source = slot_maps(owner_list, lax.axis_size("rows"), slot_count)
-    gathered = lax.all_gather(master.astype(jnp.bfloat16), "rows", axis=0, tiled=True)
+
+    def _lead_copies(chunk):
+        comm_axis = "rows"
+        base_arr, found_now = (lax.axis_size(comm_axis), lax.axis_index(comm_axis))
+        piece_out, field_out = (chunk, 1)
+        while field_out < base_arr:
+            state_now = lax.ppermute(
+                piece_out,
+                axis_name=comm_axis,
+                perm=tuple(((ii, ii ^ field_out) for ii in range(base_arr))),
+            )
+            all_values = jnp.concatenate([piece_out, state_now], 0)
+            tall = jnp.concatenate([state_now, piece_out], 0)
+            piece_out = jnp.where(found_now & field_out == 0, all_values, tall)
+            field_out = 2 * field_out
+        return piece_out
+
+    gathered = _lead_copies(master.astype(jnp.bfloat16))
     buckets = jnp.take(gathered, bucket_place, axis=0)
     weight_table = buckets.reshape(-1, channels)[:PR]
     w_in = weight_table[:FF]

time: 556 us -> 682 us (1.23)
  waiting for transfers between devices: 130 us -> 223 us
  other arithmetic: 136 us -> 150 us
  starting transfers between devices: 12.2 us -> 23.6 us
  local copies, waits for them, and re-layouts: 133 us -> 141 us
    ppermute x0 -> x3, waiting for transfers between devices: none -> 117 us  [_lead_copies(): lax.ppermute(piece_out, axis_name=comm_axis, perm=tuple(((ii, ii ^ field_...]
    all_gather x1 -> x0, waiting for transfers between devices: 25.9 us -> none  [local(): lax.all_gather(master.astype(jnp.bfloat16), 'rows', axis=0, tiled=True)]
    select_n x0 -> x3, other arithmetic: none -> 10.1 us  [_lead_copies(): piece_out = jnp.where(found_now & field_out == 0, all_values, tall)]
    ppermute x0 -> x3, starting transfers between devices: none -> 7.23 us  [_lead_copies(): lax.ppermute(piece_out, axis_name=comm_axis, perm=tuple(((ii, ii ^ field_...]
    unnamed x159 -> x183, local copies, waits for them, and re-layouts: 17.5 us -> 18.9 us
  transfers between devices with their start and end apart: 8 -> 10, of which waited for: 2 -> 3; matrix products, arithmetic and copies ran while one was open for 28% -> 25% of each run, Pallas kernels for 0% -> 0%
where the time goes in v1:
time: 682 us; the launch traced here: 672 us
  waiting for transfers between devices  223 us (33%)
  other arithmetic  150 us (22%)
  local copies, waits for them, and re-layouts  141 us (21%)
  matrix products  119 us (17%)
  starting transfers between devices  23.6 us (3%)
  between operations  15.7 us (2%)
    ppermute x3, waiting for transfers between devices, _lead_copies(): lax.ppermute(piece_out, axis_name=comm_axis, perm=tuple(((ii, ii ^ field_...  117 us
    dot_general x11, matrix products, contract(): lax.dot_general(left_side, right_side, (((left_dim,), (right_dim,)), ((),...  109 us
    psum x1, waiting for transfers between devices, local(): summed = lax.psum(grad_buckets, ('rows', 'seq'))  106 us
    another operation x3, other arithmetic  41.5 us
    concatenate x1, local copies, waits for them, and re-layouts, local(): jnp.concatenate([grad_w_in, grad_w_out, grad_w_head, vec_grads, in_rows,...  27.3 us
    add x1, other arithmetic, local(): input_grad + conv_weight[tap_index] * keep * halo_grad[:, begin:begin + f...  20.7 us
    unnamed x183, local copies, waits for them, and re-layouts  18.9 us
    reshape x1, local copies, waits for them, and re-layouts, local(): signal.reshape(rows_here, frames_here, lap_count, HOP)  14.4 us
  transfers between devices with their start and end apart: 10, of which 3 were waited for; matrix products, arithmetic and copies ran while one was open for 25% of the time, Pallas kernels for 0%

profile of v1, /device:TPU:0, one launch (start us, length us, event | category | flops | bytes accessed | tf_op | source)
XLA Modules:
  0.0 671.7 jit_solution(8410640900672271529)
XLA Ops:
  7.2 2.5 convert_element_type.160
  9.7 2.9 collective-permute-start
  14.0 2.0 collective-permute-start.3
  19.8 2.7 reshape.271
  22.5 2.2 copy.33
  25.4 2.7 fusion.48
  30.9 2.7 reshape.270
  33.7 2.2 copy.31
  35.9 2.4 maximum_select_fusion.2
  41.1 2.2 fusion.47
  43.2 34.7 %collective-permute-done.1 = bf16[54,32,512]{2,1,0:T(8,128)(2,1)S(1)} collective-permute-done((bf16[54,32,512]{2,1,0:T(8,128)(2,1)S(1)}, bf16[54,32,512]{2,1,0:T(8,128)(2,1)S(1)}, u32[]{:S(2)}, u32[]{:S(2)}) %collective-permute-start.1) | collective-permute-done | bytes 1769504 | tf_op jit(solution)/shard_map/ppermute | solution.py:126
  78.5 2.7 collective-permute-start.2
  82.6 15.2 %multiply_convert_fusion.2 = (bf16[641,1280]{1,0:T(8,128)(2,1)}, bf16[641,1280]{1,0:T(8,128)(2,1)}) fusion(f32[641]{0:T(1024)S(1)} %fusion.74, f32[641]{0:T(1024)S(1)} %select_multiply_fusion), kind=kLoop, calls=%fused_computation.91 | loop fusion | flops 10666240 | bytes 3287048 | tf_op jit(solution)/shard_map/convert.12
  101.0 13.6 %concatenate.59 = bf16[2,1030,512]{2,1,0:T(8,128)(2,1)} concatenate(bf16[2,3,512]{2,1,0:T(4,128)(2,1)} %collective-permute-done.3, bf16[2,1024,512]{2,1,0:T(8,128)(2,1)} %param.8, bf16[2,3,512]{2,1,0:T(4,128)(2,1)} %collective-permute-done.4), dimensions={1} | concatenate | bytes 4218880 | tf_op jit(solution)/shard_map/concatenate | solution.py:40
  114.6 4.3 convert_element_type.164
  119.0 4.7 fusion.55
  123.8 3.2 pad_maximum_fusion.1
  126.9 10.2 %copy.34 = bf16[2,1024,4,320]{1,0,3,2:T(2,128)(2,1)} copy(bf16[2,1024,4,320]{1,3,0,2:T(8,128)(2,1)} %pad_maximum_fusion.1) | data formatting | bytes 10485760 | tf_op jit(solution)/shard_map/stack | solution.py:233
  137.2 4.8 copy.39
  142.0 9.7 %fusion.49 = f32[2048,1282]{0,1:T(8,128)} fusion(bf16[2048,1280]{0,1:T(8,128)(2,1)S(1)} %bitcast.122, bf16[641,1280]{1,0:T(8,128)(2,1)S(1)} %copy-done.22, bf16[641,1280]{1,0:T(8,128)(2,1)S(1)} %copy-done.23), kind=kOutput, calls=%fused_computation.124 | convolution fusion | flops 6727936000 | bytes 19026944 | tf_op jit(solution)/shard_map/dot_general | solution.py:104
  151.7 82.5 %collective-permute-done.2 = bf16[108,32,512]{2,1,0:T(8,128)(2,1)} collective-permute-done((bf16[108,32,512]{2,1,0:T(8,128)(2,1)S(1)}, bf16[108,32,512]{2,1,0:T(8,128)(2,1)}, u32[]{:S(2)}, u32[]{:S(2)}) %collective-permute-start.2) | collective-permute-done | bytes 3538976 | tf_op jit(solution)/shard_map/ppermute | solution.py:126
  234.2 7.1 %maximum_select_fusion = bf16[216,32,512]{2,1,0:T(8,128)(2,1)} fusion(bf16[108,32,512]{2,1,0:T(8,128)(2,1)} %collective-permute-done.2, bf16[108,32,512]{2,1,0:T(8,128)(2,1)S(1)} %maximum_select_fusion.1, pred[]{:T(512)S(6)} %eq.134), kind=kLoop, calls=%fused_computation.23 | loop fusion | flops 10616832 | bytes 14155777 | tf_op jit(solution)/shard_map/jit(_where)/select_n | solution.py:133
  241.3 10.7 %gather_fusion = bf16[137,32,512]{2,1,0:T(8,128)(2,1)} fusion(bf16[216,32,512]{2,1,0:T(8,128)(2,1)} %maximum_select_fusion, s32[1024]{0:T(1024)} %pad_clamp_fusion.1), kind=kCustom, calls=%fused_computation | custom fusion | bytes 8978980 | tf_op jit(solution)/shard_map/jit(_take)/gather | solution.py:138
  252.1 4.2 bitcast_select_fusion
  256.3 2.6 broadcast_select_fusion
  259.1 2.4 slice-done
  261.5 6.1 fusion.88
  268.6 2.4 bitcast_subtract_fusion
  271.0 2.5 fusion.60
  273.5 2.3 fusion.89
  276.6 4.0 add_convert_fusion.3
  280.7 31.4 %multiply_convert_fusion = (bf16[2048,1536]{1,0:T(8,128)(2,1)S(1)}, f32[2048,1536]{1,0:T(8,128)}, f32[2048,1536]{1,0:T(8,128)}) fusion(f32[1536]{0:T(1024)S(1)} %reshape.280, bf16[2048,512]{1,0:T(8,128)(2,1)S(1)} %add_convert_fusion.3, bf16[1536,512]{1,0:T(8,128)(2,1)S(1)} %bitcast.123), kind=kOutput, calls=%fused_computation.6 | convolution fusion | flops 3428843520 | bytes 35133440 | tf_op jit(solution)/shard_map/dot_general | solution.py:104
  312.1 5.5 fusion.86
  317.7 1.9 copy-done.8
  320.5 5.8 convolution_add_fusion
  326.3 24.2 %add_convert_fusion.1 = (bf16[2048,641]{0,1:T(8,128)(2,1)S(1)}, bf16[2048,641]{0,1:T(8,128)(2,1)S(1)}, bf16[2048,641]{0,1:T(8,128)(2,1)}, bf16[2048,641]{0,1:T(8,128)(2,1)}) fusion(f32[2048,1282]{0,1:T(8,128)} %fusion.49, f32[2048,1282]{0,1:T(8,128)S(1)} %convolution_add_fusion), kind=kLoop, calls=%fused_computation.32 | loop fusion | flops 15753216 | bytes 31506432 | tf_op jit(solution)/shard_map/convert.2
  352.7 6.2 multiply_reduce_fusion
  358.9 4.6 fusion.52
  363.6 2.0 fusion.85
  368.4 3.6 fusion.95
  372.0 16.5 %convert_reduce_fusion = (f32[1536]{0:T(1024)S(1)}, bf16[2048,1536]{1,0:T(8,128)(2,1)}) fusion(f32[2048,1536]{1,0:T(8,128)} %get-tuple-element.33, bf16[2048,512]{1,0:T(8,128)(2,1)} %copy-done.21, bf16[1536,512]{1,0:T(8,128)(2,1)} %bitcast.126, f32[2048,1536]{1,0:T(8,128)} %get-tuple-element.84, f32[1536]{0:T(1024)S(1)} %reshape.280), kind=kOutput, calls=%fused_computation.4 | convolution fusion | flops 3274701312 | bytes 35139584 | tf_op jit(solution)/shard_map/dot_general | solution.py:104
  388.5 6.7 multiply_reduce_fusion.9
  395.2 5.1 fusion.94
  400.4 2.2 fusion.27
  404.3 5.5 fusion.84
  410.4 3.2 slice-done.2
  413.6 5.3 multiply_reduce_fusion.2
  418.9 27.3 %concatenate.66 = f32[4380,512]{1,0:T(8,128)} concatenate(f32[1536,512]{1,0:T(8,128)} %fusion.94, f32[1536,512]{1,0:T(8,128)S(1)} %fusion.95, f32[1282,512]{1,0:T(8,128)} %fusion.52, f32[1,512]{1,0:T(1,128)S(1)} %bitcast.156, f32[1,512]{1,0:T(1,128)S(1)} %bitcast.155, f32[1,512]{1,0:T(1,128)S(1)} %bitcast.154, f32[1,512]{1,0:T(1,128)S(1)} %bitcast.153, f32[1,512]{1,0:T(1,128)S(1)} %bitcast.152, ...), dimensions={0} | concatenate | bytes 17940480 | tf_op jit(solution)/shard_map/concatenate | solution.py:310
  446.2 8.1 %pad.35 = f32[4384,512]{1,0:T(8,128)} pad(f32[4380,512]{1,0:T(8,128)} %concatenate.66, f32[]{:T(128)} %constant.46.clone.1), padding=0_4x0_0 | pad | bytes 17948676 | tf_op jit(solution)/shard_map/jit(_pad)/pad | solution.py:313
  456.1 13.5 %fusion.6 = f32[2048,1280]{0,1:T(8,128)} fusion(bf16[2048,641]{0,1:T(8,128)(2,1)} %get-tuple-element.41, bf16[2048,641]{0,1:T(8,128)(2,1)S(1)} %copy-done.17, bf16[641,1280]{1,0:T(8,128)(2,1)} %get-tuple-element.91, bf16[641,1280]{1,0:T(8,128)(2,1)} %get-tuple-element.92), kind=kOutput, calls=%fused_computation.35 | convolution fusion | flops 6738438144 | bytes 19018752 | tf_op jit(solution)/shard_map/dot_general | solution.py:104
  469.6 14.4 %reshape.268 = f32[2,1024,4,320]{1,0,3,2:T(2,128)} reshape(f32[2048,1280]{0,1:T(8,128)} %fusion.6) | data formatting | bytes 20971520 | tf_op jit(solution)/shard_map/reshape | solution.py:206
  484.0 8.6 %copy_multiply_fusion = f32[2,1024,4,320]{1,3,0,2:T(8,128)S(1)} fusion(f32[2,1024,4,320]{1,0,3,2:T(2,128)} %reshape.268, f32[4,320]{1,0:T(4,128)S(1)} %copy-done.58), kind=kLoop, calls=%fused_computation.21 | loop fusion | flops 2621440 | bytes 20976640 | tf_op jit(solution)/shard_map/mul | solution.py:206
  493.0 1.8 fusion.46
  495.2 2.5 collective-permute-start.5
  497.7 2.3 pad_add_fusion
  502.1 7.9 %collective-permute-start.8 = (f32[2,3,512]{2,1,0:T(4,128)S(1)}, f32[2,3,512]{2,1,0:T(4,128)S(1)}, u32[]{:S(2)}, u32[]{:S(2)}) collective-permute-start(f32[2,3,512]{2,1,0:T(4,128)S(1)} %get-tuple-element.50), channel_id=1, source_target_pairs={{0,1},{1,2},{2,3},{4,5},{5,6},{6,7},{8,9},{9,10},{10,11},{12,13},{... | collective-permute-start | bytes 36872 | tf_op jit(solution)/shard_map/ppermute | solution.py:36
  510.0 2.4 fusion.43
  512.5 2.3 copy.30
  514.8 4.1 reshape.269
  519.0 20.7 %fusion.13 = f32[2,1024,512]{2,1,0:T(8,128)} fusion(f32[2,3,512]{2,1,0:T(4,128)S(1)} %collective-permute-done.8, f32[2,3,512]{2,1,0:T(4,128)S(1)} %collective-permute-done.7, f32[2,1024,512]{2,1,0:T(8,128)} %bitcast.119, f32[2,1024,512]{2,1,0:T(8,128)} %bitcast.118, f32[512]{0:T(512)S(1)} %bitcast.135, f32[2,1024]{1,0:T(2,128)S(1)} %copy-done.36, ...), kind=kLoop, calls=%fused_computation.47 | loop fusion | flops 27262976 | bytes 12670976 | tf_op jit(solution)/shard_map/add | solution.py:296
  539.7 105.8 %all-reduce.10.cloned.1.call-done = f32[137,32,512]{2,1,0:T(8,128)} async-done(((f32[137,32,512]{2,1,0:T(8,128)}), f32[137,32,512]{2,1,0:T(8,128)}) %all-reduce.10.cloned.1.call-update) | async-done | bytes 8978448 | tf_op jit(solution)/shard_map/psum | solution.py:315
  645.5 9.1 %concatenate.67 = f32[138,32,512]{2,1,0:T(8,128)} pad(f32[137,32,512]{2,1,0:T(8,128)} %all-reduce.10.cloned.1.call-done, f32[]{:T(128)} %constant.46.clone.1), padding=0_1x0_0x0_0 | pad | bytes 18022404 | tf_op jit(solution)/shard_map/concatenate | solution.py:316
  654.6 4.5 gather_fusion.1
  659.1 5.5 multiply_subtract_fusion
  (250 shorter events, 31.0 us)
Async XLA Ops:
  7.2 638.3 %all-reduce.10.cloned.1.call-start = ((), (), s32[]{:S(2)}) async-start(), calls=%async_computation | async-start | bytes 17956864 | tf_op jit(solution)/shard_map/psum | solution.py:315
  9.7 26.1 %collective-permute-start = (bf16[27,32,512]{2,1,0:T(8,128)(2,1)}, bf16[27,32,512]{2,1,0:T(8,128)(2,1)}, u32[]{:S(2)}, u32[]{:S(2)}) collective-permute-start(bf16[27,32,512]{2,1,0:T(8,128)(2,1)} %convert_element_type.160), channel_id=1, source_target_pairs={{0,4},{4,0},{8,12},{12,8},{16,20},{20,16},{24,28},{28,24},{1,5},{5... | collective-permute-start | bytes 2654216 | tf_op jit(solution)/shard_map/ppermute | solution.py:126
  14.0 87.0 %collective-permute-start.3 = (bf16[2,3,512]{2,1,0:T(4,128)(2,1)}, bf16[2,3,512]{2,1,0:T(4,128)(2,1)}, u32[]{:S(2)}, u32[]{:S(2)}) collective-permute-start(bf16[2,3,512]{2,1,0:T(4,128)(2,1)} %get-tuple-element.55), channel_id=1, source_target_pairs={{0,1},{1,2},{2,3},{4,5},{5,6},{6,7},{8,9},{9,10},{10,11},{12,13},{... | collective-permute-start | bytes 18440 | tf_op jit(solution)/shard_map/ppermute | solution.py:36
  16.1 85.0 %collective-permute-start.4 = (bf16[2,3,512]{2,1,0:T(4,128)(2,1)}, bf16[2,3,512]{2,1,0:T(4,128)(2,1)}, u32[]{:S(2)}, u32[]{:S(2)}) collective-permute-start(bf16[2,3,512]{2,1,0:T(4,128)(2,1)} %get-tuple-element.54), channel_id=1, source_target_pairs={{1,0},{2,1},{3,2},{5,4},{6,5},{7,6},{9,8},{10,9},{11,10},{13,12},{... | collective-permute-start | bytes 18440 | tf_op jit(solution)/shard_map/ppermute | solution.py:39
  19.7 21.2 %copy-start.50 = (f32[320]{0:T(512)}, f32[320]{0:T(512)S(1)}, u32[]{:S(2)}) copy-start(f32[320]{0:T(512)S(1)} %get-tuple-element.75) | copy-start | bytes 3844
  19.7 21.3 %copy-start.52 = (f32[320]{0:T(512)}, f32[320]{0:T(512)S(1)}, u32[]{:S(2)}) copy-start(f32[320]{0:T(512)S(1)} %get-tuple-element.76) | copy-start | bytes 3844
  19.7 21.3 %copy-start.54 = (f32[320]{0:T(512)}, f32[320]{0:T(512)S(1)}, u32[]{:S(2)}) copy-start(f32[320]{0:T(512)S(1)} %get-tuple-element.77) | copy-start | bytes 3844
  19.7 21.3 %copy-start.56 = (f32[320]{0:T(512)}, f32[320]{0:T(512)S(1)}, u32[]{:S(2)}) copy-start(f32[320]{0:T(512)S(1)} %get-tuple-element.78) | copy-start | bytes 3844
  25.4 15.6 %copy-start.26 = (f32[2,1024]{1,0:T(2,128)}, f32[2,1024]{1,0:T(2,128)S(1)}, u32[]{:S(2)}) copy-start(f32[2,1024]{1,0:T(2,128)S(1)} %get-tuple-element.68) | copy-start | bytes 24580
  25.4 15.7 %copy-start.29 = (f32[2,1024]{1,0:T(2,128)}, f32[2,1024]{1,0:T(2,128)S(1)}, u32[]{:S(2)}) copy-start(f32[2,1024]{1,0:T(2,128)S(1)} %get-tuple-element.72) | copy-start | bytes 24580
  25.4 15.7 %copy-start.32 = (f32[2,1024]{1,0:T(2,128)}, f32[2,1024]{1,0:T(2,128)S(1)}, u32[]{:S(2)}) copy-start(f32[2,1024]{1,0:T(2,128)S(1)} %get-tuple-element.73) | copy-start | bytes 24580
  29.7 89.3 %collective-permute-start.6 = (f32[2,3,320]{1,2,0:T(8,128)}, f32[2,3,320]{1,2,0:T(8,128)}, u32[]{:S(2)}, u32[]{:S(2)}) collective-permute-start(f32[2,3,320]{1,2,0:T(8,128)} %slice.387), channel_id=1, source_target_pairs={{1,0},{2,1},{3,2},{5,4},{6,5},{7,6},{9,8},{10,9},{11,10},{13,12},{... | collective-permute-start | bytes 23048 | tf_op jit(solution)/shard_map/ppermute | solution.py:47
  33.6 6.3 copy-start.74
  35.9 5.2 copy-start.12
  38.3 39.7 %collective-permute-start.1 = (bf16[54,32,512]{2,1,0:T(8,128)(2,1)S(1)}, bf16[54,32,512]{2,1,0:T(8,128)(2,1)S(1)}, u32[]{:S(2)}, u32[]{:S(2)}) collective-permute-start(bf16[54,32,512]{2,1,0:T(8,128)(2,1)S(1)} %maximum_select_fusion.2), channel_id=1, source_target_pairs={{0,8},{4,12},{8,0},{12,4},{16,24},{20,28},{24,16},{28,20},{1,9},{5... | collective-permute-start | bytes 5308424 | tf_op jit(solution)/shard_map/ppermute | solution.py:126
  40.1 58.2 %copy-start.78 = (pred[137]{0:T(512)(128)(4,1)}, pred[137]{0:T(512)(128)(4,1)S(1)}, u32[]{:S(2)}) copy-start(pred[137]{0:T(512)(128)(4,1)S(1)} %get-tuple-element.36) | copy-start | bytes 415
  43.2 39.3 %copy-start.81 = (s32[2,4]{1,0:T(2,128)S(1)}, s32[2,4]{1,0:T(2,128)}, u32[]{:S(2)}) copy-start(s32[2,4]{1,0:T(2,128)} %param.10) | copy-start | bytes 100
  78.5 155.6 %collective-permute-start.2 = (bf16[108,32,512]{2,1,0:T(8,128)(2,1)S(1)}, bf16[108,32,512]{2,1,0:T(8,128)(2,1)}, u32[]{:S(2)}, u32[]{:S(2)}) collective-permute-start(bf16[108,32,512]{2,1,0:T(8,128)(2,1)S(1)} %maximum_select_fusion.1), channel_id=1, source_target_pairs={{0,16},{4,20},{8,24},{12,28},{16,0},{20,4},{24,8},{28,12},{1,17},{... | collective-permute-start | bytes 10616840 | tf_op jit(solution)/shard_map/ppermute | solution.py:126
  114.6 4.4 copy-start.75
  114.6 4.4 copy-start.76
  114.6 4.4 copy-start.77
  118.9 4.8 copy-start.14
  137.2 4.8 copy-start.22
  137.2 4.8 copy-start.23
  241.3 10.7 %copy-start.59 = (pred[4384]{0:T(1024)(128)(4,1)S(1)}, pred[4384]{0:T(1024)(128)(4,1)}, u32[]{:S(2)}) copy-start(pred[4384]{0:T(1024)(128)(4,1)} %broadcast_in_dim.52) | copy-start | bytes 13156
  256.2 14.7 %copy-start.15 = (bf16[4384,512]{1,0:T(8,128)(2,1)}, bf16[4384,512]{1,0:T(8,128)(2,1)S(1)}, u32[]{:S(2)}) copy-start(bf16[4384,512]{1,0:T(8,128)(2,1)S(1)} %bitcast_select_fusion) | copy-start | bytes 13467652
  256.3 5.3 slice-start
  256.3 5.2 slice-start.1
  256.3 5.2 copy-start.27
  256.3 5.2 copy-start.30
  256.3 5.2 copy-start.33
  256.3 5.2 copy-start.40
  259.0 8.6 %copy-start.60 = (f32[1,512]{1,0:T(1,128)}, f32[1,512]{1,0:T(1,128)S(1)}, u32[]{:S(2)}) copy-start(f32[1,512]{1,0:T(1,128)S(1)} %get-tuple-element.59) | copy-start | bytes 6148
  259.0 8.6 %copy-start.62 = (f32[1,512]{1,0:T(1,128)}, f32[1,512]{1,0:T(1,128)S(1)}, u32[]{:S(2)}) copy-start(f32[1,512]{1,0:T(1,128)S(1)} %get-tuple-element.60) | copy-start | bytes 6148
  259.0 8.6 %copy-start.64 = (f32[1,512]{1,0:T(1,128)}, f32[1,512]{1,0:T(1,128)S(1)}, u32[]{:S(2)}) copy-start(f32[1,512]{1,0:T(1,128)S(1)} %get-tuple-element.61) | copy-start | bytes 6148
  259.0 8.6 %copy-start.66 = (f32[1,512]{1,0:T(1,128)}, f32[1,512]{1,0:T(1,128)S(1)}, u32[]{:S(2)}) copy-start(f32[1,512]{1,0:T(1,128)S(1)} %get-tuple-element.62) | copy-start | bytes 6148
  259.0 8.6 %copy-start.68 = (f32[1,512]{1,0:T(1,128)}, f32[1,512]{1,0:T(1,128)S(1)}, u32[]{:S(2)}) copy-start(f32[1,512]{1,0:T(1,128)S(1)} %get-tuple-element.63) | copy-start | bytes 6148
  259.0 8.6 %copy-start.70 = (f32[1,512]{1,0:T(1,128)}, f32[1,512]{1,0:T(1,128)S(1)}, u32[]{:S(2)}) copy-start(f32[1,512]{1,0:T(1,128)S(1)} %get-tuple-element.64) | copy-start | bytes 6148
  259.1 8.6 %copy-start.72 = (f32[1,512]{1,0:T(1,128)}, f32[1,512]{1,0:T(1,128)S(1)}, u32[]{:S(2)}) copy-start(f32[1,512]{1,0:T(1,128)S(1)} %get-tuple-element.65) | copy-start | bytes 6148
  268.6 7.2 %copy-start.44 = (f32[2048]{0:T(1024)}, f32[2048]{0:T(1024)S(1)}, u32[]{:S(2)}) copy-start(f32[2048]{0:T(1024)S(1)} %bitcast_rsqrt_fusion) | copy-start | bytes 24580
  276.6 35.4 %copy-start.25 = (bf16[48,32,512]{2,1,0:T(8,128)(2,1)}, bf16[48,32,512]{2,1,0:T(8,128)(2,1)S(1)}, u32[]{:S(2)}) copy-start(bf16[48,32,512]{2,1,0:T(8,128)(2,1)S(1)} %get-tuple-element.45) | copy-start | bytes 4718596
  280.6 31.4 %copy-start.19 = (bf16[2048,512]{1,0:T(8,128)(2,1)}, bf16[2048,512]{1,0:T(8,128)(2,1)S(1)}, u32[]{:S(2)}) copy-start(bf16[2048,512]{1,0:T(8,128)(2,1)S(1)} %add_convert_fusion.3) | copy-start | bytes 6291460
  280.7 31.4 %copy-start.18 = (bf16[2,1024,512]{2,1,0:T(8,128)(2,1)S(1)}, bf16[2,1024,512]{2,1,0:T(8,128)(2,1)}, u32[]{:S(2)}) copy-start(bf16[2,1024,512]{2,1,0:T(8,128)(2,1)} %param.8) | copy-start | bytes 6291460
  312.1 5.6 copy-start.83
  366.4 5.6 copy-start.5
  367.1 4.9 copy-start.21
  372.0 16.5 %copy-start.4 = (f32[2048,512]{1,0:T(8,128)S(1)}, f32[2048,512]{1,0:T(8,128)}, u32[]{:S(2)}) copy-start(f32[2048,512]{1,0:T(8,128)} %bitcast_subtract_fusion) | copy-start | bytes 12582916
  372.0 16.5 %copy-start.6 = (f32[2048,512]{1,0:T(8,128)S(1)}, f32[2048,512]{1,0:T(8,128)}, u32[]{:S(2)}) copy-start(f32[2048,512]{1,0:T(8,128)} %fusion.60) | copy-start | bytes 12582916
  388.5 6.7 copy-start.20
  388.5 6.7 copy-start.82
  395.2 7.3 %copy-start.7 = (f32[2048,512]{1,0:T(8,128)}, f32[2048,512]{1,0:T(8,128)S(1)}, u32[]{:S(2)}) copy-start(f32[2048,512]{1,0:T(8,128)S(1)} %get-tuple-element.88) | copy-start | bytes 12582916
  395.2 5.1 copy-start.43
  395.2 5.1 copy-start.45
  410.3 8.6 %copy-start.2 = (f32[2048,512]{1,0:T(8,128)}, f32[2048,512]{1,0:T(8,128)S(1)}, u32[]{:S(2)}) copy-start(f32[2048,512]{1,0:T(8,128)S(1)} %get-tuple-element.25) | copy-start | bytes 12582916
  469.6 14.4 %copy-start.58 = (f32[4,320]{1,0:T(4,128)S(1)}, f32[4,320]{1,0:T(4,128)}, u32[]{:S(2)}) copy-start(f32[4,320]{1,0:T(4,128)} %multiply_subtract_fusion.2) | copy-start | bytes 15364
  495.1 14.9 %copy-start.51 = (f32[320]{0:T(512)S(1)}, f32[320]{0:T(512)}, u32[]{:S(2)}) copy-start(f32[320]{0:T(512)} %copy-done.50) | copy-start | bytes 3844
  495.1 14.9 %copy-start.53 = (f32[320]{0:T(512)S(1)}, f32[320]{0:T(512)}, u32[]{:S(2)}) copy-start(f32[320]{0:T(512)} %copy-done.52) | copy-start | bytes 3844
  495.1 14.9 %copy-start.55 = (f32[320]{0:T(512)S(1)}, f32[320]{0:T(512)}, u32[]{:S(2)}) copy-start(f32[320]{0:T(512)} %copy-done.54) | copy-start | bytes 3844
  495.1 14.9 %copy-start.57 = (f32[320]{0:T(512)S(1)}, f32[320]{0:T(512)}, u32[]{:S(2)}) copy-start(f32[320]{0:T(512)} %copy-done.56) | copy-start | bytes 3844
  495.2 14.8 %collective-permute-start.5 = (f32[2,3,320]{1,2,0:T(8,128)S(1)}, f32[2,3,320]{1,2,0:T(8,128)S(1)}, u32[]{:S(2)}, u32[]{:S(2)}) collective-permute-start(f32[2,3,320]{1,2,0:T(8,128)S(1)} %pad_add_fusion.1), channel_id=1, source_target_pairs={{0,1},{1,2},{2,3},{4,5},{5,6},{6,7},{8,9},{9,10},{10,11},{12,13},{... | collective-permute-start | bytes 23048 | tf_op jit(solution)/shard_map/ppermute | solution.py:47
  500.8 18.1 %collective-permute-start.7 = (f32[2,3,512]{2,1,0:T(4,128)S(1)}, f32[2,3,512]{2,1,0:T(4,128)S(1)}, u32[]{:S(2)}, u32[]{:S(2)}) collective-permute-start(f32[2,3,512]{2,1,0:T(4,128)S(1)} %get-tuple-element.49), channel_id=1, source_target_pairs={{1,0},{2,1},{3,2},{5,4},{6,5},{7,6},{9,8},{10,9},{11,10},{13,12},{... | collective-permute-start | bytes 36872 | tf_op jit(solution)/shard_map/ppermute | solution.py:39
  502.1 16.8 %collective-permute-start.8 = (f32[2,3,512]{2,1,0:T(4,128)S(1)}, f32[2,3,512]{2,1,0:T(4,128)S(1)}, u32[]{:S(2)}, u32[]{:S(2)}) collective-permute-start(f32[2,3,512]{2,1,0:T(4,128)S(1)} %get-tuple-element.50), channel_id=1, source_target_pairs={{0,1},{1,2},{2,3},{4,5},{5,6},{6,7},{8,9},{9,10},{10,11},{12,13},{... | collective-permute-start | bytes 36872 | tf_op jit(solution)/shard_map/ppermute | solution.py:36
  539.7 119.4 %copy-start.80 = (pred[27]{0:T(512)(128)(4,1)S(1)}, pred[27]{0:T(512)(128)(4,1)}, u32[]{:S(2)}) copy-start(pred[27]{0:T(512)(128)(4,1)} %get-tuple-element.18) | copy-start | bytes 85
  654.6 4.5 copy-start.13
  (36 other events, 121.3 us)
Sparse Core Ops, SparseCore 0:
  454.5 190.9 all-reduce.9
